TPU v7x, 512 devices: a whole 4x4x16 slice. The times are simulated.
512 devices in a mesh: group: 32 (over x_lo, z), rep: 8 (over y, core), tp: 2 (over x_hi).
Axes of the slice: x: 4 (x_hi: 2, x_lo: 2; x = x_hi * 2 + x_lo), y: 4, z: 16, core: 2. Of those that a mesh axis runs over, the one named last changes fastest.
Arguments:
- prompt_states: bfloat16 [4096, 4, 8192], P('group', None, 'rep'), may hold values from -6 to 6
- kv_weight: bfloat16 [8192, 2, 1024], P('rep', None, 'tp'), may hold values from -0.0625 to 0.0625
- queries: bfloat16 [1024, 8, 8192], P(('group', 'rep'), None, 'tp'), may hold values from -600 to 600
- new_kv: bfloat16 [1024, 8, 2, 1024], P(('group', 'rep'), None, None, 'tp'), may hold values from -6 to 6
- prompt_pages: int32 [4], replicated, may hold values from 16 to 32, as said below
- decoder_prompt: int32 [32], replicated, may hold values from 0 to 3, as said below
- sample_count: int32 [32], P('group'), may hold values from 1 to 32, as said below
Outputs:
- attention_out: bfloat16 [1024, 8, 8192], P(('group', 'rep'), None, 'tp')
Inputs may be any that keep to these rules, and one draw needn't show every extreme that they name: `prompt_pages`: some prompt has all 32 pages. `decoder_prompt`: each prompt is sampled by exactly 32 // 4 decode groups. `sample_count`: some group has all its sample rows live.
All inputs are finite; a program needn't handle non-finite values.
Results may differ from a plain program's by a relative error of at most 0.013.
Values may be sent and summed in bfloat16 or wider, within the bound.
A program may use at most 64 MiB of HBM per device.

v0:
```python
import jax
import jax.numpy as jnp
from jax import lax
from jax.sharding import PartitionSpec as P

QH = 64
KVH = 8
HD = 128
PAGE = 128
STEPS = 8
S_DEV = 4


def fresh_state(query_rows, new_keys, new_values, factor):
    scores = (
        jnp.einsum("hsagd,sbhd->hsagb", query_rows, new_keys, preferred_element_type=jnp.float32)
        * factor
    )
    steps_here = scores.shape[-1]
    causal = jnp.arange(steps_here)[:, None] >= jnp.arange(steps_here)[None, :]
    causal = causal[None, None, :, None, :]
    row_max = jnp.max(jnp.where(causal, scores, -jnp.inf), axis=-1)
    weights = jnp.where(causal, jnp.exp(scores - row_max[..., None]), 0.0)
    weight_sum = jnp.sum(weights, axis=-1)
    weighted = jnp.einsum(
        "hsagb,sbhd->hsagd",
        weights.astype(jnp.bfloat16),
        new_values,
        preferred_element_type=jnp.float32,
    )
    local_heads = query_rows.shape[0]
    head_size = query_rows.shape[-1]
    return (
        row_max.reshape(local_heads, -1),
        weight_sum.reshape(local_heads, -1),
        weighted.reshape(local_heads, -1, head_size),
    )


def absorb(carry_state, query_flat, key_rows, value_rows, key_live, factor):
    row_max, weight_sum, weighted = carry_state
    scores = (
        jnp.einsum("hrd,nhd->hrn", query_flat, key_rows, preferred_element_type=jnp.float32)
        * factor
    )
    masked = jnp.where(key_live, scores, -jnp.inf)
    new_max = jnp.maximum(row_max, jnp.max(masked, axis=-1))
    weights = jnp.where(key_live, jnp.exp(scores - new_max[..., None]), 0.0)
    shrink = jnp.exp(row_max - new_max)
    weight_sum = weight_sum * shrink + jnp.sum(weights, axis=-1)
    weighted = weighted * shrink[..., None] + jnp.einsum(
        "hrn,nhd->hrd", weights.astype(jnp.bfloat16), value_rows, preferred_element_type=jnp.float32
    )
    return (new_max, weight_sum, weighted)


def absorb_all(carry_state, query_flat, key_rows, value_rows, positions, key_limit, factor):
    key_count = key_rows.shape[0]
    block_keys = min(key_count, 1024)
    for first_key in range(0, key_count, block_keys):
        last_key = min(first_key + block_keys, key_count)
        carry_state = absorb(
            carry_state,
            query_flat,
            key_rows[first_key:last_key],
            value_rows[first_key:last_key],
            positions[first_key:last_key] < key_limit,
            factor,
        )
    return carry_state


def body(prompt_states, kv_weight, queries, new_kv, prompt_pages, decoder_prompt, sample_count):
    local_heads = KVH // lax.axis_size("tp")
    query_group = QH // KVH
    factor = HD ** (-0.5)
    token_block = prompt_states.shape[0]
    prompt_total = prompt_states.shape[1]
    partial_value = jnp.dot(
        prompt_states.reshape(token_block * prompt_total, prompt_states.shape[2]),
        kv_weight.reshape(kv_weight.shape[0], 2 * local_heads * HD),
        preferred_element_type=jnp.float32,
    )
    partial_value = partial_value.reshape(token_block, prompt_total, 2 * local_heads * HD)
    summed = lax.psum(partial_value, "rep")
    kv_cache = summed.astype(jnp.bfloat16)
    chooser = (decoder_prompt[:, None] == jnp.arange(prompt_total)[None, :]).astype(jnp.bfloat16)
    outgoing = jnp.einsum(
        "gp,tpc->gtc", chooser, kv_cache, preferred_element_type=jnp.float32
    ).astype(jnp.bfloat16)
    group_index = lax.axis_index("group")
    own_prompt = decoder_prompt[group_index]
    key_limit = prompt_pages[own_prompt] * PAGE
    query_rows = queries.reshape(S_DEV, STEPS, local_heads, query_group, HD).transpose(
        2, 0, 1, 3, 4
    )
    new_parts = new_kv.reshape(S_DEV, STEPS, 2, local_heads, HD)
    running = fresh_state(query_rows, new_parts[:, :, 0], new_parts[:, :, 1], factor)
    query_flat = query_rows.reshape(local_heads, -1, HD)
    arrived = lax.all_to_all(outgoing, "group", split_axis=0, concat_axis=0, tiled=True)
    key_value = arrived.reshape(-1, 2, local_heads, HD)
    positions = jnp.arange(key_value.shape[0])
    running = absorb_all(
        running, query_flat, key_value[:, 0], key_value[:, 1], positions, key_limit, factor
    )
    row_max, weight_sum, weighted = running
    result = weighted / weight_sum[..., None]
    result = (
        result.reshape(local_heads, S_DEV, STEPS, query_group, HD)
        .transpose(1, 2, 0, 3, 4)
        .reshape(S_DEV, STEPS, -1)
    )
    replica = lax.axis_index("rep")
    row_live = jnp.arange(S_DEV) * lax.axis_size("rep") + replica < sample_count[0]
    return jnp.where(row_live[:, None, None], result, 0.0).astype(jnp.bfloat16)


def solution(mesh):
    placed = (
        P("group", None, "rep"),
        P("rep", None, "tp"),
        P(("group", "rep"), None, "tp"),
        P(("group", "rep"), None, None, "tp"),
        P(),
        P(),
        P("group"),
    )
    return jax.shard_map(
        body, mesh=mesh, in_specs=placed, out_specs=P(("group", "rep"), None, "tp"), check_vma=False
    )
```

profile of v0, /device:TPU:1, one launch (start us, length us, event | category | flops | bytes accessed | tf_op | source)
XLA Modules:
  0.0 490.1 jit_solution(15196278102294833875)
XLA Ops:
  0.0 0.0 copy-start.3
  0.0 4.5 reshape.189
  4.5 0.0 copy-done.3
  4.5 0.0 copy-start.2
  4.5 2.9 fusion.32
  7.4 57.7 %all-reduce.1 = bf16[128,4,1024]{2,0,1:T(8,128)(2,1)S(1)} all-reduce(f32[128,4,1024]{2,0,1:T(8,128)S(1)} %fusion.32), channel_id=1, replica_groups=mesh['group'=32,'rep'=8,'tp'=2] {'rep'}, use_global_device_ids=true, to_apply=%region_1.2 | all-reduce | flops 524288 | bytes 3145728 | tf_op jit(solution)/shard_map/psum | solution.py:85
  65.2 0.0 copy-done.2
  65.2 4.7 convolution_convert_fusion
  69.9 11.3 %copy.41 = bf16[32,128,1024]{2,1,0:T(8,128)(2,1)} copy(bf16[32,128,1024]{2,0,1:T(8,128)(2,1)} %convolution_convert_fusion) | data formatting | bytes 16777216 | tf_op jit(solution)/shard_map/convert_element_type | solution.py:90
  81.2 0.0 copy-start
  81.2 0.0 copy-start.1
  81.2 0.0 copy-start.4
  81.2 11.4 %all-to-all-start = ((bf16[32,128,1024]{2,1,0:T(8,128)(2,1)}), bf16[32,128,1024]{2,1,0:T(8,128)(2,1)}, u32[]{:S(2)}, u32[]{:S(2)}) async-start(bf16[32,128,1024]{2,1,0:T(8,128)(2,1)} %copy.41), calls=%async_computation | async-start | bytes 16777216 | tf_op jit(solution)/shard_map/all_to_all | solution.py:100
  92.6 0.6 dynamic_slice.6
  94.5 0.0 copy-done
  94.5 0.0 copy-done.1
  94.6 1.3 select_reduce_fusion.4
  95.9 0.1 reshape.180
  96.0 0.2 fusion.35
  96.3 0.1 reshape.184
  97.7 0.0 copy-done.4
  97.7 0.6 dynamic_slice.7
  99.0 0.3 fusion.37
  99.3 355.7 %all-to-all-done = bf16[32,128,1024]{2,1,0:T(8,128)(2,1)} async-done(((bf16[32,128,1024]{2,1,0:T(8,128)(2,1)}), bf16[32,128,1024]{2,1,0:T(8,128)(2,1)}, u32[]{:S(2)}, u32[]{:S(2)}) %all-to-all-start) | async-done | bytes 8388640 | tf_op jit(solution)/shard_map/all_to_all | solution.py:100
  455.0 14.3 %reshape.193 = bf16[4096,2,4,128]{3,2,1,0:T(4,128)(2,1)} reshape(bf16[32,128,1024]{2,1,0:T(8,128)(2,1)} %all-to-all-done) | data formatting | bytes 16777216 | tf_op jit(solution)/shard_map/reshape | solution.py:101
  469.3 5.1 %fusion.57 = (bf16[1024,1,4,128]{3,2,1,0:T(4,128)(2,1)S(1)}, bf16[1024,1,4,128]{3,2,1,0:T(4,128)(2,1)S(1)}, bf16[1024,1,4,128]{3,2,1,0:T(4,128)(2,1)S(1)}, bf16[...) fusion(bf16[4096,2,4,128]{3,2,1,0:T(4,128)(2,1)} %reshape.193), kind=kLoop, calls=%fused_computation.99 | loop fusion | bytes 16777216 | tf_op jit(solution)/shard_map/slice | solution.py:66
  474.4 1.3 select_reduce_fusion
  475.7 1.3 select_reduce_fusion.1
  477.1 1.3 select_reduce_fusion.2
  478.4 1.5 select_reduce_fusion.3
  480.0 0.9 bitcast_reduce_fusion.3
  480.8 0.9 bitcast_reduce_fusion.2
  481.7 0.9 bitcast_reduce_fusion.1
  482.6 0.9 bitcast_reduce_fusion
  483.5 0.2 bitcast_multiply_fusion
  483.7 1.4 fusion.24
  485.1 1.4 fusion.25
  486.4 1.4 fusion.26
  487.8 1.4 fusion.34
  489.3 0.8 select_convert_fusion
  (10 shorter events, 0.2 us)
Async XLA Ops:
  0.0 4.5 copy-start.3
  4.5 60.6 %copy-start.2 = (s32[32]{0:T(128)S(1)}, s32[32]{0:T(128)}, u32[]{:S(2)}) copy-start(s32[32]{0:T(128)} %param.12) | copy-start | bytes 388
  81.2 13.3 %copy-start = (bf16[4,8,4096]{2,1,0:T(8,128)(2,1)S(1)}, bf16[4,8,4096]{2,1,0:T(8,128)(2,1)}, u32[]{:S(2)}) copy-start(bf16[4,8,4096]{2,1,0:T(8,128)(2,1)} %param.9) | copy-start | bytes 786436
  81.2 13.3 %copy-start.1 = (bf16[4,8,2,512]{3,2,1,0:T(2,128)(2,1)S(1)}, bf16[4,8,2,512]{3,2,1,0:T(2,128)(2,1)}, u32[]{:S(2)}) copy-start(bf16[4,8,2,512]{3,2,1,0:T(2,128)(2,1)} %param.10) | copy-start | bytes 196612
  81.2 16.4 %copy-start.4 = (s32[4]{0:T(128)S(1)}, s32[4]{0:T(128)}, u32[]{:S(2)}) copy-start(s32[4]{0:T(128)} %param.11) | copy-start | bytes 52
  81.2 373.7 %all-to-all-start = ((bf16[32,128,1024]{2,1,0:T(8,128)(2,1)}), bf16[32,128,1024]{2,1,0:T(8,128)(2,1)}, u32[]{:S(2)}, u32[]{:S(2)}) async-start(bf16[32,128,1024]{2,1,0:T(8,128)(2,1)} %copy.41), calls=%async_computation | async-start | bytes 16777216 | tf_op jit(solution)/shard_map/all_to_all | solution.py:100
where the time goes:
time: 498 us; the launch traced here: 490 us
  waiting for transfers between devices  356 us (71%)
  blocking collectives  57.7 us (12%)
  local copies, waits for them, and re-layouts  36.8 us (7%)
  matrix products  20.3 us (4%)
  starting transfers between devices  11.4 us (2%)
    all_to_all x1, waiting for transfers between devices, body(): lax.all_to_all(outgoing, 'group', split_axis=0, concat_axis=0, tiled=True)  356 us
    psum x1, blocking collectives, body(): summed = lax.psum(partial_value, 'rep')  57.7 us
    reshape x1, local copies, waits for them, and re-layouts, body(): key_value = arrived.reshape(-1, 2, local_heads, HD)  14.3 us
    all_to_all x1, starting transfers between devices, body(): lax.all_to_all(outgoing, 'group', split_axis=0, concat_axis=0, tiled=True)  11.4 us
    convert_element_type x1, local copies, waits for them, and re-layouts, body(): outgoing = jnp.einsum('gp,tpc->gtc', chooser, kv_cache, preferred_element...  11.3 us
  transfers between devices with their start and end apart: 1, of which 1 were waited for; matrix products, arithmetic and copies ran while one was open for 1% of the time, Pallas kernels for 0%

commit v1 on v0

v1 whole, which is shorter than its diff:
```python
import functools

import jax
import jax.numpy as jnp
from jax import lax
from jax.experimental import pallas as pl
from jax.experimental.pallas import tpu as pltpu
from jax.sharding import PartitionSpec as P

MESH = pl.DeviceIdType.MESH
F32 = jnp.float32
BF16 = jnp.bfloat16

HD = 128
PAGE = 128
QG = 8
STEPS = 8
S_DEV = 4
NX = 2
NY = 4
PROMPTS = 4
CHUNKS = 4
TOK = PAGE // CHUNKS
ROWS = TOK * PROMPTS
HALF = ROWS // 2
QROWS = QG * S_DEV * STEPS
SCALE = HD**-0.5 * 1.4426950408889634


def kernel(
    nz,
    x_hbm,
    w_hbm,
    q_hbm,
    n_hbm,
    pages_ref,
    dec_ref,
    cnt_ref,
    o_hbm,
    xv,
    wv,
    nv,
    wr,
    part,
    pair,
    ra,
    sb,
    rb,
    fin,
    unit,
    land,
    picked,
    kv,
    qrec,
    nstage,
    nrec,
    qs,
    acc,
    mx,
    ostage,
    in_sem,
    pair_s,
    pair_r,
    ra_s,
    ra_r,
    rb_s,
    rb_r,
    z_s,
    z_r,
    x_s,
    x_r,
    c_s,
    c_r,
    f_s,
    f_r,
    q_s,
    q_r,
    n_s,
    n_r,
    o_s,
    o_r,
    l_s,
):
    last = nz // 2
    g = lax.axis_index("group")
    r = lax.axis_index("rep")
    cx = g // nz
    z = g % nz
    y = r // 2
    k = r % 2
    turn = 1 - 2 * k
    to_a = {"group": cx * nz + (z + turn + nz) % nz}
    to_b = {"group": cx * nz + (z - turn + nz) % nz}
    to_x = {"group": (1 - cx) * nz + z}
    to_core = {"rep": y * 2 + 1 - k}
    y_opp, y_up, y_dn = (y + 2) % NY, (y + 1) % NY, (y + 3) % NY
    to_opp = {"rep": y_opp * 2 + k}
    to_up = {"rep": y_up * 2 + k}
    to_dn = {"rep": y_dn * 2 + k}

    def remote(src, dst, ss, rs, to):
        return pltpu.make_async_remote_copy(
            src_ref=src, dst_ref=dst, send_sem=ss, recv_sem=rs, device_id=to, device_id_type=MESH
        )

    get_w = pltpu.make_async_copy(w_hbm, wv, in_sem.at[0])
    get_x = pltpu.make_async_copy(x_hbm, xv, in_sem.at[1])
    get_n = pltpu.make_async_copy(n_hbm, nv, in_sem.at[2])
    get_w.start()
    get_x.start()
    get_n.start()

    everyone = (to_a, to_b, to_x, to_core, to_opp, to_up, to_dn)
    barrier = pltpu.get_barrier_semaphore()
    for other in everyone:
        pl.semaphore_signal(barrier, inc=1, device_id=other, device_id_type=MESH)
    pl.semaphore_wait(barrier, len(everyone))

    def pair_copy(j):
        return remote(part.at[j, 1 - k], pair.at[j], pair_s.at[j], pair_r.at[j], to_core)

    def ra_copies(j):
        h0, h1 = pl.ds(0, HALF), pl.ds(HALF, HALF)
        plan = (
            (y_opp, h0, 0, to_up),
            (y_up, h1, 1, to_up),
            (y_opp, h1, 2, to_dn),
            (y_dn, h0, 3, to_dn),
        )
        return [
            remote(part.at[j, k, head, rows], ra.at[j, i], ra_s.at[j, i], ra_r.at[j, i], to)
            for head, rows, i, to in plan
        ]

    def rb_copies(j):
        return [
            remote(sb.at[j, i], rb.at[j, i], rb_s.at[j, i], rb_r.at[j, i], to)
            for i, to in ((0, to_up), (1, to_dn))
        ]

    def z_copy(way, s, j):
        src = unit.at[j] if isinstance(s, int) and s == 1 else land.at[way, s - 2, j]
        return remote(
            src, land.at[way, s - 1, j], z_s.at[way, s - 1, j], z_r.at[way, s - 1, j],
            to_a if way == 0 else to_b,
        )

    def z_arrival(way, s, j):
        return remote(
            unit.at[j], land.at[way, s - 1, j], z_s.at[way, s - 1, j], z_r.at[way, s - 1, j],
            to_a if way == 0 else to_b,
        )

    def x_copy(s, n):
        return remote(
            picked.at[s, pl.ds(0, n)], kv.at[k, s, cx, pl.ds(0, n)], x_s.at[s], x_r.at[s], to_x
        )

    def own_copy(s, n):
        here = kv.at[k, s, cx, pl.ds(0, n)]
        return remote(here, here, c_s.at[s], c_r.at[s], to_core)

    def fwd_copy(s, n):
        here = kv.at[k, s, 1 - cx, pl.ds(0, n)]
        return remote(here, here, f_s.at[s], f_r.at[s], to_core)

    def x_arrival(s, n):
        return remote(
            picked.at[s, pl.ds(0, n)], kv.at[k, s, 1 - cx, pl.ds(0, n)], x_s.at[s], x_r.at[s], to_x
        )

    def own_arrival(s, n):
        there = kv.at[1 - k, s, cx, pl.ds(0, n)]
        return remote(there, there, c_s.at[s], c_r.at[s], to_core)

    def fwd_arrival(s, n):
        there = kv.at[1 - k, s, 1 - cx, pl.ds(0, n)]
        return remote(there, there, f_s.at[s], f_r.at[s], to_core)

    ways = ((y_opp, to_opp, 0), (y_up, to_up, 2), (y_dn, to_dn, 1))

    def q_copies():
        return [
            remote(
                q_hbm.at[:, pl.ds(pl.multiple_of(yy * QG * HD, QG * HD), QG * HD)],
                qrec.at[slot], q_s.at[i], q_r.at[slot], to,
            )
            for i, (yy, to, slot) in enumerate(ways)
        ]

    def n_copies():
        return [
            remote(nstage.at[yy], nrec.at[slot], n_s.at[i], n_r.at[slot], to)
            for i, (yy, to, slot) in enumerate(ways)
        ]

    my_columns = pl.ds(pl.multiple_of(y * QG * HD, QG * HD), QG * HD)
    q_own = pltpu.make_async_copy(q_hbm.at[:, my_columns], qrec.at[3], l_s.at[0])
    n_own = pltpu.make_async_copy(nstage.at[y], nrec.at[3], l_s.at[1])
    o_own = pltpu.make_async_copy(ostage.at[3], o_hbm.at[:, my_columns], l_s.at[2])

    mine = dec_ref[g]
    theirs = dec_ref[(1 - cx) * nz + z]
    limit = pages_ref[mine]
    count = cnt_ref[0]

    def choose(blocks, which):
        out = blocks[3]
        for p in (2, 1, 0):
            out = jnp.where(which == p, blocks[p], out)
        return out

    def pick(blocks, s, pos, j):
        rows = pl.ds(j * TOK, TOK)
        kv[k, s, cx, pos, rows, :] = choose(blocks, mine)
        picked[s, pos, rows, :] = choose(blocks, theirs)

    def project(j):
        rows = xv[pl.ds(j * TOK, TOK)].reshape(ROWS, xv.shape[2])
        got = jnp.dot(rows, wr[...], preferred_element_type=F32)
        for kind in range(2):
            for h in range(NY):
                first = (kind * NY + h) * HD
                part[j, kind, h] = got[:, first : first + HD]
        pair_copy(j).start()

    def sum_pair(j):
        pair_copy(j).wait_recv()
        for h in range(NY):
            part[j, k, h] = part[j, k, h] + pair[j, h]
        for copy in ra_copies(j):
            copy.start()

    def sum_next(j):
        for copy in ra_copies(j):
            copy.wait_recv()
        sb[j, 0] = part[j, k, y_up, pl.ds(0, HALF), :] + ra[j, 0]
        sb[j, 1] = part[j, k, y_dn, pl.ds(HALF, HALF), :] + ra[j, 2]
        for copy in rb_copies(j):
            copy.start()

    def sum_last(j):
        for copy in rb_copies(j):
            copy.wait_recv()
        fin[j, pl.ds(0, HALF), :] = part[j, k, y, pl.ds(0, HALF), :] + ra[j, 3] + rb[j, 0]
        fin[j, pl.ds(HALF, HALF), :] = part[j, k, y, pl.ds(HALF, HALF), :] + ra[j, 1] + rb[j, 1]
        blocks = []
        for p in range(PROMPTS):
            block = fin[j, pl.ds(p, TOK, stride=PROMPTS), :].astype(BF16)
            unit[j, p] = block
            blocks.append(block)
        z_copy(0, 1, j).start()
        z_copy(1, 1, j).start()
        pick(blocks, 0, 0, j)

    get_w.wait()
    wr[...] = wv[...].reshape(wr.shape)
    get_x.wait()
    for t in range(CHUNKS + 3):
        if t < CHUNKS:
            project(t)
        if 0 <= t - 1 < CHUNKS:
            sum_pair(t - 1)
        if 0 <= t - 2 < CHUNKS:
            sum_next(t - 2)
        if 0 <= t - 3 < CHUNKS:
            sum_last(t - 3)
        if t == 0:
            get_n.wait()
            flat = nv[...].reshape(S_DEV * STEPS, nv.shape[2] * nv.shape[3])
            for h in range(NY):
                for kind in range(2):
                    first = (kind * NY + h) * HD
                    nstage[h, kind] = flat[:, first : first + HD]
            q_own.start()
            n_own.start()
        if t == CHUNKS:
            for copy in q_copies() + n_copies():
                copy.start()
    x_copy(0, 1).start()
    own_copy(0, 1).start()

    def begin(i):
        for h in range(QG):
            qs[i, pl.ds(h * S_DEV * STEPS, S_DEV * STEPS), :] = qrec[i, :, pl.ds(h * HD, HD)]
        keys, values = nrec[i, 0], nrec[i, 1]
        scores = lax.dot_general(
            qs[i], keys, (((1,), (1,)), ((), ())), preferred_element_type=F32
        )
        row = lax.broadcasted_iota(jnp.int32, scores.shape, 0)
        col = lax.broadcasted_iota(jnp.int32, scores.shape, 1)
        row_step, col_step = row % STEPS, col % STEPS
        same = (row // STEPS) % S_DEV == col // STEPS
        scores = jnp.where(same & (col_step <= row_step), scores, -jnp.inf)
        top = jnp.max(scores, axis=1, keepdims=True)
        weights = jnp.exp2((scores - top) * SCALE)
        wide = jnp.concatenate([values, jnp.ones_like(values)], axis=1)
        acc[i] = jnp.dot(weights.astype(BF16), wide, preferred_element_type=F32)
        mx[i] = jnp.broadcast_to(top, (QROWS, HD))

    def attend(s, i, both):
        if both:
            keys = kv[0, s].reshape(4 * PAGE, HD)
            values = jnp.concatenate([kv[1, s, c, pos] for c in range(2) for pos in (1, 0)], axis=0)
            sources = ((z - s + nz) % nz, (z + s) % nz)
        else:
            keys = jnp.concatenate([kv[0, s, c, 0] for c in range(2)], axis=0)
            values = jnp.concatenate([kv[1, s, c, 0] for c in range(2)], axis=0)
            sources = ((z + s) % nz,)
        scores = lax.dot_general(
            qs[i], keys, (((1,), (1,)), ((), ())), preferred_element_type=F32
        )
        width = len(sources) * PAGE
        pieces = [scores[:, :width]]
        for n, source in enumerate(sources):
            piece = scores[:, width + n * PAGE : width + (n + 1) * PAGE]
            pieces.append(jnp.where(nz + source < limit, piece, -jnp.inf))
        scores = jnp.concatenate(pieces, axis=1)
        before = mx[i][:, :1]
        top = jnp.maximum(before, jnp.max(scores, axis=1, keepdims=True))
        shrink = jnp.exp2((before - top) * SCALE)
        weights = jnp.exp2((scores - top) * SCALE)
        wide = jnp.concatenate([values, jnp.ones_like(values)], axis=1)
        acc[i] = acc[i] * shrink + jnp.dot(weights.astype(BF16), wide, preferred_element_type=F32)
        mx[i] = jnp.broadcast_to(top, (QROWS, HD))

    def ready(s, n):
        own_arrival(s, n).wait_recv()
        fwd_arrival(s, n).wait_recv()

    def pass_on(s, n):
        x_arrival(s, n).wait_recv()
        fwd_copy(s, n).start()

    def hop(s, j):
        z_arrival(0, s, j).wait_recv()
        z_copy(0, s + 1, j).start()
        z_arrival(1, s, j).wait_recv()

        @pl.when(s < last - 1)
        def _():
            z_copy(1, s + 1, j).start()

        for way in range(2):
            pick([land[way, s - 1, j, p] for p in range(PROMPTS)], s, way, j)

    def hop_done(s):
        x_copy(s, 2).start()
        own_copy(s, 2).start()

    q_own.wait()
    n_own.wait()
    for copy in q_copies() + n_copies():
        copy.wait_recv()

    def first_step(j, carry):
        hop(1, j)
        begin(j)
        return carry

    lax.fori_loop(0, CHUNKS, first_step, 0)
    pass_on(0, 1)
    hop_done(1)

    ready(0, 1)

    def second_step(j, carry):
        hop(2, j)
        attend(0, j, False)
        return carry

    lax.fori_loop(0, CHUNKS, second_step, 0)
    pass_on(1, 2)
    hop_done(2)

    def later_step(s, carry):
        ready(s - 2, 2)

        def inner(j, c):
            hop(s, j)
            attend(s - 2, j, True)
            return c

        lax.fori_loop(0, CHUNKS, inner, 0)
        pass_on(s - 1, 2)
        hop_done(s)
        return carry

    lax.fori_loop(3, last, later_step, 0)

    ready(last - 2, 2)

    def last_step(j, carry):
        z_arrival(0, last, j).wait_recv()
        pick([land[0, last - 1, j, p] for p in range(PROMPTS)], last, 0, j)
        attend(last - 2, j, True)
        return carry

    lax.fori_loop(0, CHUNKS, last_step, 0)
    x_copy(last, 1).start()
    own_copy(last, 1).start()
    pass_on(last - 1, 2)
    pass_on(last, 1)
    ready(last - 1, 2)

    def tail_step(j, carry):
        attend(last - 1, j, True)
        return carry

    lax.fori_loop(0, CHUNKS, tail_step, 0)
    ready(last, 1)

    def o_copy(i, to):
        return remote(ostage.at[i], o_hbm.at[:, my_columns], o_s.at[i], o_r.at[i], to)

    for i, (yy, to) in enumerate(((y_opp, to_opp), (y_up, to_up), (y_dn, to_dn), (y, None))):
        attend(last, i, False)
        result = acc[i][:, :HD] / acc[i][:, HD:]
        rows = S_DEV * STEPS
        result = jnp.concatenate([result[h * rows : (h + 1) * rows] for h in range(QG)], axis=1)
        sample = lax.broadcasted_iota(jnp.int32, result.shape, 0) // STEPS
        live = sample * (NY * 2) + (yy * 2 + k) < count
        ostage[i] = jnp.where(live, result, 0.0).astype(BF16)
        if to is None:
            o_own.start()
        else:
            o_copy(i, to).start()

    for j in range(CHUNKS):
        pair_copy(j).wait_send()
        for copy in ra_copies(j) + rb_copies(j):
            copy.wait_send()

    def sent(s, carry):
        for j in range(CHUNKS):
            z_arrival(0, s, j).wait_send()

            @pl.when(s < last)
            def _():
                z_arrival(1, s, j).wait_send()

        return carry

    lax.fori_loop(1, last + 1, sent, 0)
    for s, n in ((0, 1), (last, 1)):
        x_copy(s, n).wait_send()
        own_copy(s, n).wait_send()
        fwd_copy(s, n).wait_send()

    def sent_two(s, carry):
        x_copy(s, 2).wait_send()
        own_copy(s, 2).wait_send()
        fwd_copy(s, 2).wait_send()
        return carry

    lax.fori_loop(1, last, sent_two, 0)
    for copy in q_copies() + n_copies():
        copy.wait_send()
    o_own.wait()
    for i, (yy, to) in enumerate(((y_opp, to_opp), (y_up, to_up), (y_dn, to_dn))):
        o_copy(i, to).wait_send()
        yyy = (y_opp, y_dn, y_up)[i]
        there = o_hbm.at[:, pl.ds(pl.multiple_of(yyy * QG * HD, QG * HD), QG * HD)]
        remote(ostage.at[i], there, o_s.at[i], o_r.at[i], to).wait_recv()


def body(nz, prompt_states, kv_weight, queries, new_kv, prompt_pages, decoder_prompt, sample_count):
    steps = nz // 2
    depth, width = kv_weight.shape[0], 2 * kv_weight.shape[2]
    any_space = pl.BlockSpec(memory_space=pl.ANY)
    smem = pl.BlockSpec(memory_space=pltpu.SMEM)
    rows = S_DEV * STEPS
    dma = pltpu.SemaphoreType.DMA
    out = pl.pallas_call(
        functools.partial(kernel, nz),
        out_shape=jax.ShapeDtypeStruct((rows, queries.shape[2]), BF16),
        in_specs=[any_space] * 4 + [smem] * 3,
        out_specs=any_space,
        scratch_shapes=[
            pltpu.VMEM(prompt_states.shape, BF16),
            pltpu.VMEM(kv_weight.shape, BF16),
            pltpu.VMEM(new_kv.shape, BF16),
            pltpu.VMEM((depth, width), BF16),
            pltpu.VMEM((CHUNKS, 2, NY, ROWS, HD), F32),
            pltpu.VMEM((CHUNKS, NY, ROWS, HD), F32),
            pltpu.VMEM((CHUNKS, 4, HALF, HD), F32),
            pltpu.VMEM((CHUNKS, 2, HALF, HD), F32),
            pltpu.VMEM((CHUNKS, 2, HALF, HD), F32),
            pltpu.VMEM((CHUNKS, ROWS, HD), F32),
            pltpu.VMEM((CHUNKS, PROMPTS, TOK, HD), BF16),
            pltpu.VMEM((2, steps, CHUNKS, PROMPTS, TOK, HD), BF16),
            pltpu.VMEM((steps + 1, 2, PAGE, HD), BF16),
            pltpu.VMEM((2, steps + 1, NX, 2, PAGE, HD), BF16),
            pltpu.VMEM((NY, rows, QG * HD), BF16),
            pltpu.VMEM((NY, 2, rows, HD), BF16),
            pltpu.VMEM((NY, 2, rows, HD), BF16),
            pltpu.VMEM((NY, QROWS, HD), BF16),
            pltpu.VMEM((NY, QROWS, 2 * HD), F32),
            pltpu.VMEM((NY, QROWS, HD), F32),
            pltpu.VMEM((NY, rows, QG * HD), BF16),
            dma((3,)),
            dma((CHUNKS,)),
            dma((CHUNKS,)),
            dma((CHUNKS, 4)),
            dma((CHUNKS, 4)),
            dma((CHUNKS, 2)),
            dma((CHUNKS, 2)),
            dma((2, steps, CHUNKS)),
            dma((2, steps, CHUNKS)),
            dma((steps + 1,)),
            dma((steps + 1,)),
            dma((steps + 1,)),
            dma((steps + 1,)),
            dma((steps + 1,)),
            dma((steps + 1,)),
            dma((3,)),
            dma((3,)),
            dma((3,)),
            dma((3,)),
            dma((3,)),
            dma((3,)),
            dma((3,)),
        ],
        compiler_params=pltpu.CompilerParams(
            collective_id=0, has_side_effects=True, vmem_limit_bytes=48 * 2**20
        ),
        cost_estimate=pl.CostEstimate(
            flops=6_500_000_000, bytes_accessed=4_000_000, transcendentals=4_200_000
        ),
    )(
        prompt_states,
        kv_weight,
        queries.reshape(rows, queries.shape[2]),
        new_kv,
        prompt_pages,
        decoder_prompt,
        sample_count,
    )
    return out.reshape(queries.shape)


def solution(mesh):
    placed = (
        P("group", None, "rep"),
        P("rep", None, "tp"),
        P(("group", "rep"), None, "tp"),
        P(("group", "rep"), None, None, "tp"),
        P(),
        P(),
        P("group"),
    )
    return jax.shard_map(
        functools.partial(body, mesh.shape["group"] // NX),
        mesh=mesh,
        in_specs=placed,
        out_specs=P(("group", "rep"), None, "tp"),
        check_vma=False,
    )
```

time: 498 us -> 85 us (0.17); the launches traced: 490 us -> 84.7 us
  waiting for transfers between devices: 356 us -> 0 us
  Pallas kernels: 0 us -> 77.4 us
  blocking collectives: 57.7 us -> 0 us
  local copies, waits for them, and re-layouts: 36.8 us -> 6.61 us
  matrix products: 20.3 us -> 0 us
  starting transfers between devices: 11.4 us -> 0 us
    all_to_all x1 -> x0, waiting for transfers between devices: 356 us -> none  [body(): lax.all_to_all(outgoing, 'group', split_axis=0, concat_axis=0, tiled=True)]
    pallas_call x0 -> x1, Pallas kernels: none -> 77.4 us  [body(): pl.pallas_call(functools.partial(kernel, nz), out_shape=jax.ShapeDtypeStr...]
    psum x1 -> x0, blocking collectives: 57.7 us -> none  [body(): summed = lax.psum(partial_value, 'rep')]
    dot_general x12 -> x0, matrix products: 20.3 us -> none  [the longest x4 5.53 us: absorb(): jnp.einsum('hrd,nhd->hrn', query_flat, key_rows, preferred_element_type=j...]
    reshape x6 -> x0, local copies, waits for them, and re-layouts: 19.2 us -> none  [the longest x1 14.3 us: body(): key_value = arrived.reshape(-1, 2, local_heads, HD)]
    all_to_all x1 -> x0, starting transfers between devices: 11.4 us -> none  [body(): lax.all_to_all(outgoing, 'group', split_axis=0, concat_axis=0, tiled=True)]
    convert_element_type x1 -> x0, local copies, waits for them, and re-layouts: 11.3 us -> none  [body(): outgoing = jnp.einsum('gp,tpc->gtc', chooser, kv_cache, preferred_element...]
    unnamed x10 -> x13, local copies, waits for them, and re-layouts: 0.02 us -> 6.61 us
  transfers between devices with their start and end apart: 1 -> 0, of which waited for: 1 -> 0; matrix products, arithmetic and copies ran while one was open for 1% -> 0% of each run, Pallas kernels for 0% -> 0%
where the time goes in v1:
time: 85 us; the launch traced here: 84.7 us
  Pallas kernels  77.4 us (91%)
  local copies, waits for them, and re-layouts  6.61 us (8%)
    pallas_call x1, Pallas kernels, body(): pl.pallas_call(functools.partial(kernel, nz), out_shape=jax.ShapeDtypeStr...  77.4 us
    unnamed x13, local copies, waits for them, and re-layouts  6.61 us

profile of v1, /device:TPU:1, one launch (start us, length us, event | category | flops | bytes accessed | tf_op | source)
XLA Modules:
  0.0 84.7 jit_solution(1152805397062794841)
XLA Ops:
  0.7 0.0 copy-start
  0.7 1.6 %copy-done = bf16[1024,2,512]{2,1,0:T(2,128)(2,1)S(1)} copy-done((bf16[1024,2,512]{2,1,0:T(2,128)(2,1)S(1)}, bf16[1024,2,512]{2,1,0:T(2,128)(2,1)}, u32[]{:S(2)}) %copy-start) | copy-done | bytes 2097176
  2.2 0.0 copy-start.1
  2.2 1.2 %copy-done.1 = bf16[128,4,1024]{2,1,0:T(4,128)(2,1)S(1)} copy-done((bf16[128,4,1024]{2,1,0:T(4,128)(2,1)S(1)}, bf16[128,4,1024]{2,1,0:T(4,128)(2,1)}, u32[]{:S(2)}) %copy-start.1) | copy-done | bytes 1048600
  3.5 0.0 copy-start.2
  3.5 0.9 %copy-done.2 = bf16[4,8,4096]{2,1,0:T(8,128)(2,1)S(1)} copy-done((bf16[4,8,4096]{2,1,0:T(8,128)(2,1)S(1)}, bf16[4,8,4096]{2,1,0:T(8,128)(2,1)}, u32[]{:S(2)}) %copy-start.2) | copy-done | bytes 262168
  4.4 0.0 copy-start.3
  4.4 0.8 copy-done.3
  5.3 0.0 copy-start.4
  5.3 0.7 copy-done.4
  5.9 0.0 copy-start.5
  5.9 0.7 copy-done.5
  6.6 77.4 %shard_map.73 = bf16[32,4096]{1,0:T(8,128)(2,1)S(1)} custom-call(bf16[128,4,1024]{2,1,0:T(4,128)(2,1)S(1)} %copy-done.1, bf16[1024,2,512]{2,1,0:T(2,128)(2,1)S(1)} %copy-done, bf16[32,4096]{1,0:T(8,128)(2,1)S(1)} %bitcast.3, bf16[4,8,2,512]{3,2,1,0:T(2,128)(2,1)S(1)} %copy-done.3, s32[4]{0:T(128)S(1)} %copy-done.4, s32[32]{0:T(128)S(1)} %copy-done.5, ...), custom_call_target="tpu_custom_call" | custom-call | flops 6499999744 | bytes 4000000 | tf_op jit(solution)/shard_map/pallas_call | solution.py:474
  84.0 0.7 copy.10
Async XLA Ops:
  0.7 1.6 %copy-start = (bf16[1024,2,512]{2,1,0:T(2,128)(2,1)S(1)}, bf16[1024,2,512]{2,1,0:T(2,128)(2,1)}, u32[]{:S(2)}) copy-start(bf16[1024,2,512]{2,1,0:T(2,128)(2,1)} %w_hbm.1) | copy-start | bytes 6291460
  2.2 1.2 %copy-start.1 = (bf16[128,4,1024]{2,1,0:T(4,128)(2,1)S(1)}, bf16[128,4,1024]{2,1,0:T(4,128)(2,1)}, u32[]{:S(2)}) copy-start(bf16[128,4,1024]{2,1,0:T(4,128)(2,1)} %x_hbm.1) | copy-start | bytes 3145732
  3.5 0.9 %copy-start.2 = (bf16[4,8,4096]{2,1,0:T(8,128)(2,1)S(1)}, bf16[4,8,4096]{2,1,0:T(8,128)(2,1)}, u32[]{:S(2)}) copy-start(bf16[4,8,4096]{2,1,0:T(8,128)(2,1)} %param.9) | copy-start | bytes 786436
  4.4 0.8 copy-start.3
  5.3 0.7 copy-start.4
  5.9 0.7 copy-start.5
